TPU v7x, 32 devices: a whole 2x2x4 slice. The times are simulated.
32 devices in a mesh: patch: 4 (over z), dev: 8 (over y, x, core).
Axes of the slice: x: 2, y: 2, z: 4, core: 2. Of those that a mesh axis runs over, the one named last changes fastest.
Arguments:
- measure_plane: float32 [2, 65536], P(None, ('patch', 'dev')), may hold values from -1 to 1
- measure_weight: float32 [65536], P(('patch', 'dev')), may hold values from 0.1 to 2
- measure_visit: int32 [65536], P(('patch', 'dev')), may hold values from 0 to 63
- measure_holder: int32 [65536, 1], P(('patch', 'dev')), may hold values from 0 to 7; in each aligned block of 2048 rows (0 to 2047, 2048 to 4095, ...) at most 640 rows name the same one
- measure_star: int32 [65536], P(('patch', 'dev')), may hold values from 0 to 255
- visit_coefficients: float32 [512, 56], P('dev'), may hold values from -4 to 4
- star_location: float32 [2, 8192], P(None, ('patch', 'dev')), may hold values from -6 to 6
Outputs:
- schur_blocks: float32 [512, 784], P('dev')
- schur_rhs: float32 [512, 56], P('dev')
- star_offset: float32 [2, 8192], P(None, ('patch', 'dev'))
Inputs may be any that keep to these rules, and one draw needn't show every extreme that they name: `measure_holder`: in each aligned block of 2048 rows (the rows of one device) no value appears more than 640 times.
All inputs are finite; a program needn't handle non-finite values.
Results may differ from a plain program's by a relative error of at most 0.0001.
Values sent between devices are 32-bit elements; how exact they have to be, the bound alone decides.
A program may use at most 64 MiB of HBM per device.

v0:
```python
import functools
import math

import jax
import jax.numpy as jnp
import ml_dtypes
import numpy as np
from jax import lax
from jax.experimental import pallas as pl
from jax.experimental.pallas import tpu as pltpu
from jax.sharding import PartitionSpec as P

NMON = 28
DEG = 6
PAIRS = [(a, b) for a in range(DEG + 1) for b in range(DEG + 1 - a)]
MOMENTS = 144
ROWS = 256
COLS = 1024
RHS_COL = 896
F32 = jnp.float32
BF16 = jnp.bfloat16
MESH = pl.DeviceIdType.MESH
NT = (((1,), (1,)), ((), ()))
NN = (((1,), (0,)), ((), ()))


def moment_row(p, q):
    return 16 * p + q if p <= 4 else 80 + 8 * (p - 5) + q


def expansion():
    table = np.zeros((ROWS, COLS), np.float32)
    for k, (a, b) in enumerate(PAIRS):
        for l, (c, d) in enumerate(PAIRS):
            for p in (a + c, abs(a - c)):
                for q in (b + d, abs(b - d)):
                    table[moment_row(p, q), k * NMON + l] += 0.25
        for c in range(2):
            table[MOMENTS + c * 56 + a * 8 + b, RHS_COL + c * NMON + k] = 1.0
    return table.astype(ml_dtypes.bfloat16)


def coefficient_spread():
    table = np.zeros((112, 2 * NMON), np.float32)
    for k, (a, b) in enumerate(PAIRS):
        for c in range(2):
            table[c * 56 + a * 8 + b, c * NMON + k] = 1.0
    return table.astype(ml_dtypes.bfloat16)


def split3(x):
    high = x.astype(BF16)
    rest = x - high.astype(F32)
    middle = rest.astype(BF16)
    return high, middle, (rest - middle.astype(F32)).astype(BF16)


def dot(a, b, dims):
    return lax.dot_general(a, b, dims, preferred_element_type=F32)


def three(total, rows):
    return total[:rows] + total[rows : 2 * rows] + total[2 * rows : 3 * rows]


def kernel(
    n_dev,
    n_patch,
    scale,
    plane_ref,
    weight_ref,
    visit_ref,
    holder_ref,
    star_ref,
    coef_ref,
    loc_ref,
    spread_ref,
    expand_hbm,
    blocks_ref,
    rhs_ref,
    offset_ref,
    expand_ref,
    tu_ref,
    tv_ref,
    loc_tile,
    part_ref,
    part_in,
    table_ref,
    moment_ref,
    moment_in,
    sum_ref,
    expand_sem,
    send_a,
    recv_a,
    send_b,
    recv_b,
    send_c,
    recv_c,
    send_d,
    recv_d,
):
    me_d = lax.axis_index("dev")
    me_p = lax.axis_index("patch")
    barrier = pltpu.get_barrier_semaphore()
    for j in range(1, n_dev):
        pl.semaphore_signal(
            barrier, inc=1, device_id={"dev": lax.rem(me_d + j, n_dev)}, device_id_type=MESH
        )
    for j in range(1, n_patch):
        pl.semaphore_signal(
            barrier, inc=1, device_id={"patch": lax.rem(me_p + j, n_patch)}, device_id_type=MESH
        )
    expand_copy = pltpu.make_async_copy(expand_hbm, expand_ref, expand_sem)
    expand_copy.start()

    rows = weight_ref.shape[1]
    visits = coef_ref.shape[0]
    weight = weight_ref[...]
    coords = plane_ref[...]
    series = [jnp.ones_like(coords), coords]
    for degree in range(2, 13):
        series.append(2.0 * coords * series[-1] - series[-2])
    tv_ref[...] = jnp.zeros_like(tv_ref)
    for degree, value in enumerate(series):
        tu_ref[degree : degree + 1, :] = value[0:1]
        tv_ref[degree : degree + 1, :] = value[1:2]

    def basis(a, group):
        return tu_ref[a : a + 1, :] * tv_ref[8 * group : 8 * group + 8, :]

    visit_hot = jnp.where(
        lax.broadcasted_iota(jnp.int32, (visits, rows), 0) == visit_ref[...], 1.0, 0.0
    ).astype(BF16)
    coef = jnp.concatenate(
        [dot(spread_ref[...], piece, NT) for piece in split3(coef_ref[...])], axis=0
    ).astype(BF16)
    picked = three(dot(coef, visit_hot, NN), 112)
    predicted = []
    for c in range(2):
        total = picked[c * 56 : c * 56 + 8] * basis(0, 0)
        for a in range(1, 7):
            total = total + picked[c * 56 + 8 * a : c * 56 + 8 * a + 8] * basis(a, 0)
        predicted.append(jnp.sum(total, axis=0, keepdims=True))

    star = star_ref[...]
    low = lax.rem(star, 128)
    place = holder_ref[...] * 2 + lax.div(star, 128)
    low_hot = jnp.where(
        lax.broadcasted_iota(jnp.int32, (128, rows), 0) == low, 1.0, 0.0
    ).astype(BF16)
    sub = lax.broadcasted_iota(jnp.int32, (8, rows), 0)
    half = lax.div(sub, 4)
    kind = lax.rem(sub, 4)
    values = jnp.where(
        kind == 0,
        weight,
        jnp.where(
            kind == 1,
            weight * predicted[0],
            jnp.where(kind == 2, weight * predicted[1], 0.0),
        ),
    )
    here = place - half
    masked = []
    for piece in split3(values):
        piece = piece.astype(F32)
        masked += [jnp.where(here == 2 * d, piece, 0.0) for d in range(n_dev)]
    sums = three(
        dot(jnp.concatenate(masked, axis=0).astype(BF16), low_hot, NT), 8 * n_dev
    )
    for d in range(n_dev):
        part_ref[d] = sums[8 * d : 8 * d + 8]
    loc_tile[...] = jnp.zeros_like(loc_tile)
    for h in range(2):
        for c in range(2):
            loc_tile[4 * h + 1 + c : 4 * h + 2 + c, :] = loc_ref[
                c : c + 1, 128 * h : 128 * h + 128
            ]

    pl.semaphore_wait(barrier, n_dev + n_patch - 2)
    scatter = []
    for j in range(1, n_dev):
        peer = lax.rem(me_d + j, n_dev)
        copy = pltpu.make_async_remote_copy(
            src_ref=part_ref.at[peer],
            dst_ref=part_in.at[j - 1],
            send_sem=send_a.at[j - 1],
            recv_sem=recv_a.at[j - 1],
            device_id={"dev": peer},
            device_id_type=MESH,
        )
        copy.start()
        scatter.append(copy)
    star_total = part_ref[me_d]
    for j in range(1, n_dev):
        scatter[j - 1].wait_recv()
        star_total = star_total + part_in[j - 1]

    tile_row = lax.broadcasted_iota(jnp.int32, (8, 128), 0)
    mass = jnp.where(tile_row < 4, star_total[0:1], star_total[4:5])
    floor = jnp.maximum(mass, 1.0)
    location = loc_tile[...]
    offset = (star_total - mass * location) / floor
    table_ref[me_d] = jnp.where(
        lax.rem(tile_row, 4) == 0, 1.0 / floor, location + offset
    )
    gather = []
    for j in range(1, n_dev):
        copy = pltpu.make_async_remote_copy(
            src_ref=table_ref.at[me_d],
            dst_ref=table_ref.at[me_d],
            send_sem=send_b.at[j - 1],
            recv_sem=recv_b.at[j - 1],
            device_id={"dev": lax.rem(me_d + j, n_dev)},
            device_id_type=MESH,
        )
        copy.start()
        gather.append(copy)
    for h in range(2):
        for c in range(2):
            offset_ref[c : c + 1, 128 * h : 128 * h + 128] = offset[
                4 * h + 1 + c : 4 * h + 2 + c
            ]
    for copy in gather:
        copy.wait_recv()
    table = table_ref[...].reshape(8 * n_dev, 128)
    found = three(
        dot(jnp.concatenate(split3(table), axis=0), low_hot, NN), 8 * n_dev
    )
    chosen = jnp.where(here == 0, found[0:8], 0.0)
    for d in range(1, n_dev):
        chosen = chosen + jnp.where(here == 2 * d, found[8 * d : 8 * d + 8], 0.0)
    chosen = chosen[0:4] + chosen[4:8]
    normal = weight * (1.0 - weight * chosen[0:1])
    error = [weight * (predicted[c] - chosen[1 + c : 2 + c]) for c in range(2)]

    stack = []
    for a in range(13):
        stack += [normal * basis(a, group) for group in range(2 if a <= 4 else 1)]
    for c in range(2):
        stack += [error[c] * basis(a, 0) for a in range(7)]
    pieces = jnp.concatenate(split3(jnp.concatenate(stack, axis=0)), axis=0)
    moments = three(dot(pieces, visit_hot, NT), ROWS)
    packed = jnp.concatenate([moments[:128], moments[128:]], axis=1)
    share = 128 // n_patch
    for q in range(n_patch):
        moment_ref[q] = packed[q * share : (q + 1) * share]
    scatter_p = []
    for j in range(1, n_patch):
        peer = lax.rem(me_p + j, n_patch)
        copy = pltpu.make_async_remote_copy(
            src_ref=moment_ref.at[peer],
            dst_ref=moment_in.at[j - 1],
            send_sem=send_c.at[j - 1],
            recv_sem=recv_c.at[j - 1],
            device_id={"patch": peer},
            device_id_type=MESH,
        )
        copy.start()
        scatter_p.append(copy)
    total = moment_ref[me_p]
    for j in range(1, n_patch):
        scatter_p[j - 1].wait_recv()
        total = total + moment_in[j - 1]
    sum_ref[me_p] = total
    gather_p = []
    for j in range(1, n_patch):
        copy = pltpu.make_async_remote_copy(
            src_ref=sum_ref.at[me_p],
            dst_ref=sum_ref.at[me_p],
            send_sem=send_d.at[j - 1],
            recv_sem=recv_d.at[j - 1],
            device_id={"patch": lax.rem(me_p + j, n_patch)},
            device_id_type=MESH,
        )
        copy.start()
        gather_p.append(copy)
    expand_copy.wait()
    for copy in gather_p:
        copy.wait_recv()
    turned = sum_ref[...].reshape(128, 128).T
    left = jnp.concatenate(split3(turned[:visits]), axis=0)
    right = jnp.concatenate(split3(turned[visits:]), axis=0)
    result = three(
        dot(left, expand_ref[:128, :], NN) + dot(right, expand_ref[128:, :], NN), visits
    )
    blocks_ref[...] = result[:, : NMON * NMON] * scale
    rhs_ref[...] = result[:, RHS_COL : RHS_COL + 2 * NMON] * math.sqrt(scale)
    for copy in scatter + gather + scatter_p + gather_p:
        copy.wait_send()


def per_device(n_dev, n_patch, plane, weight, visit, holder, star, coef, loc):
    rows = weight.shape[0]
    visits = coef.shape[0]
    scale = visits / (rows * n_patch)
    share = 128 // n_patch
    vmem = pl.BlockSpec(memory_space=pltpu.VMEM)
    dma = pltpu.SemaphoreType.DMA
    return tuple(
        pl.pallas_call(
            functools.partial(kernel, n_dev, n_patch, scale),
            out_shape=(
                jax.ShapeDtypeStruct((visits, NMON * NMON), F32),
                jax.ShapeDtypeStruct((visits, 2 * NMON), F32),
                jax.ShapeDtypeStruct(loc.shape, F32),
            ),
            in_specs=[vmem] * 8 + [pl.BlockSpec(memory_space=pl.ANY)],
            out_specs=(vmem, vmem, vmem),
            scratch_shapes=[
                pltpu.VMEM((ROWS, COLS), BF16),
                pltpu.VMEM((16, rows), F32),
                pltpu.VMEM((16, rows), F32),
                pltpu.VMEM((8, 128), F32),
                pltpu.VMEM((n_dev, 8, 128), F32),
                pltpu.VMEM((n_dev - 1, 8, 128), F32),
                pltpu.VMEM((n_dev, 8, 128), F32),
                pltpu.VMEM((n_patch, share, 128), F32),
                pltpu.VMEM((n_patch - 1, share, 128), F32),
                pltpu.VMEM((n_patch, share, 128), F32),
                dma,
                dma((n_dev - 1,)),
                dma((n_dev - 1,)),
                dma((n_dev - 1,)),
                dma((n_dev - 1,)),
                dma((n_patch - 1,)),
                dma((n_patch - 1,)),
                dma((n_patch - 1,)),
                dma((n_patch - 1,)),
            ],
            compiler_params=pltpu.CompilerParams(
                collective_id=0, has_side_effects=True, vmem_limit_bytes=40 * 1024 * 1024
            ),
        )(
            plane,
            weight.reshape(1, rows),
            visit.reshape(1, rows),
            holder.reshape(1, rows),
            star.reshape(1, rows),
            coef,
            loc,
            jnp.asarray(coefficient_spread()),
            jnp.asarray(expansion()),
        )
    )


def solution(mesh):
    placed = (
        P(None, ("patch", "dev")),
        P(("patch", "dev")),
        P(("patch", "dev")),
        P(("patch", "dev"), None),
        P(("patch", "dev")),
        P("dev", None),
        P(None, ("patch", "dev")),
    )
    return jax.shard_map(
        functools.partial(per_device, mesh.shape["dev"], mesh.shape["patch"]),
        mesh=mesh,
        in_specs=placed,
        out_specs=(P("dev", None), P("dev", None), P(None, ("patch", "dev"))),
        check_vma=False,
    )
```

profile of v0, /device:TPU:0, one launch (start us, length us, event | category | flops | bytes accessed | tf_op | source)
XLA Modules:
  0.0 27.6 jit_solution(15070077430713374273)
XLA Ops:
  0.6 0.0 copy-start.7
  0.6 0.0 copy-start.1
  0.7 0.0 copy-start.2
  0.7 0.0 copy-start.3
  0.7 0.0 copy-start.4
  0.7 0.8 %copy.12.coef_ref = f32[64,56]{1,0:T(8,128)S(1)} copy(f32[64,56]{0,1:T(8,128)} %param.14) | data formatting | bytes 28672 | tf_op args[5]
  1.5 0.0 copy-done.7
  1.5 0.0 copy-done.1
  1.6 0.0 copy-done.2
  1.6 0.0 copy-done.3
  1.6 0.0 copy-done.4
  1.6 0.0 copy-start
  1.6 1.0 %copy-done = bf16[256,1024]{1,0:T(8,128)(2,1)S(1)} copy-done((bf16[256,1024]{1,0:T(8,128)(2,1)S(1)}, bf16[256,1024]{1,0:T(8,128)(2,1)}, u32[]{:S(2)}) %copy-start) | copy-done | bytes 524312
  2.6 0.0 copy-start.5
  2.6 0.7 %copy-done.5 = s32[2048,1]{0,1:T(1,128)S(1)} copy-done((s32[2048,1]{0,1:T(1,128)S(1)}, s32[2048,1]{0,1:T(1,128)}, u32[]{:S(2)}) %copy-start.5) | copy-done | bytes 8216
  3.3 0.0 copy-start.6
  3.3 0.7 %copy-done.6 = s32[2048]{0:T(1024)S(1)} copy-done((s32[2048]{0:T(1024)S(1)}, s32[2048]{0:T(1024)}, u32[]{:S(2)}) %copy-start.6) | copy-done | bytes 8216
  4.0 21.7 %shard_map.112 = (f32[64,784]{1,0:T(8,128)S(1)}, f32[64,56]{1,0:T(8,128)S(1)}, f32[2,256]{1,0:T(2,128)S(1)}) custom-call(f32[2,2048]{1,0:T(2,128)S(1)} %copy-done.2, f32[1,2048]{1,0:T(1,128)S(1)} %bitcast.4, s32[1,2048]{1,0:T(1,128)S(1)} %bitcast.5, s32[1,2048]{1,0:T(1,128)S(1)} %bitcast.6, s32[1,2048]{1,0:T(1,128)S(1)} %bitcast.7, ...), custom_call_target="tpu_custom_call" | custom-call | tf_op jit(solution)/shard_map/pallas_call | solution.py:301
  25.7 0.7 %copy.13 = f32[64,56]{0,1:T(8,128)} copy(f32[64,56]{1,0:T(8,128)S(1)} %get-tuple-element.4) | data formatting | bytes 28672 | tf_op jit(solution)/shard_map/pallas_call | solution.py:301
  26.4 0.7 %copy.16 = f32[64,784]{1,0:T(8,128)} copy(f32[64,784]{1,0:T(8,128)S(1)} %get-tuple-element.9) | data formatting | bytes 401408
  27.1 0.6 %copy.17 = f32[2,256]{1,0:T(2,128)} copy(f32[2,256]{1,0:T(2,128)S(1)} %get-tuple-element.11) | data formatting | bytes 4096
Async XLA Ops:
  0.6 0.9 %copy-start.7 = (f32[2,256]{1,0:T(2,128)S(1)}, f32[2,256]{1,0:T(2,128)}, u32[]{:S(2)}) copy-start(f32[2,256]{1,0:T(2,128)} %loc_ref.1) | copy-start | bytes 6148
  0.6 0.9 %copy-start.1 = (bf16[112,56]{1,0:T(8,128)(2,1)S(1)}, bf16[112,56]{1,0:T(8,128)(2,1)}, u32[]{:S(2)}) copy-start(bf16[112,56]{1,0:T(8,128)(2,1)} %constant.4.clone.spread_ref) | copy-start | bytes 37636
  0.7 0.9 %copy-start.2 = (f32[2,2048]{1,0:T(2,128)S(1)}, f32[2,2048]{1,0:T(2,128)}, u32[]{:S(2)}) copy-start(f32[2,2048]{1,0:T(2,128)} %plane_ref.1) | copy-start | bytes 49156
  0.7 0.9 %copy-start.3 = (f32[2048]{0:T(1024)S(1)}, f32[2048]{0:T(1024)}, u32[]{:S(2)}) copy-start(f32[2048]{0:T(1024)} %param.10) | copy-start | bytes 24580
  0.7 0.9 %copy-start.4 = (s32[2048]{0:T(1024)S(1)}, s32[2048]{0:T(1024)}, u32[]{:S(2)}) copy-start(s32[2048]{0:T(1024)} %param.11) | copy-start | bytes 24580
  1.6 1.0 %copy-start = (bf16[256,1024]{1,0:T(8,128)(2,1)S(1)}, bf16[256,1024]{1,0:T(8,128)(2,1)}, u32[]{:S(2)}) copy-start(bf16[256,1024]{1,0:T(8,128)(2,1)} %constant.5.clone.expand_hbm) | copy-start | bytes 1572868
  2.6 0.7 %copy-start.5 = (s32[2048,1]{0,1:T(1,128)S(1)}, s32[2048,1]{0,1:T(1,128)}, u32[]{:S(2)}) copy-start(s32[2048,1]{0,1:T(1,128)} %param.12) | copy-start | bytes 24580
  3.3 0.7 %copy-start.6 = (s32[2048]{0:T(1024)S(1)}, s32[2048]{0:T(1024)}, u32[]{:S(2)}) copy-start(s32[2048]{0:T(1024)} %param.13) | copy-start | bytes 24580
where the time goes:
time: 28 us; the launch traced here: 27.6 us
  Pallas kernels  21.7 us (78%)
  local copies, waits for them, and re-layouts  5.26 us (19%)
  between operations  0.73 us (3%)
    pallas_call x1, Pallas kernels, per_device(): pl.pallas_call(functools.partial(kernel, n_dev, n_patch, scale), out_shap...  21.7 us
    unnamed x19, local copies, waits for them, and re-layouts  4.57 us
    pallas_call x1, local copies, waits for them, and re-layouts, per_device(): pl.pallas_call(functools.partial(kernel, n_dev, n_patch, scale), out_shap...  0.69 us

commit v1 on v0

v1 whole, which is shorter than its diff:
```python
import functools
import math

import jax
import jax.numpy as jnp
import ml_dtypes
import numpy as np
from jax import lax
from jax.experimental import pallas as pl
from jax.experimental.pallas import tpu as pltpu
from jax.sharding import PartitionSpec as P

NMON = 28
DEG = 6
PAIRS = [(a, b) for a in range(DEG + 1) for b in range(DEG + 1 - a)]
MOMENTS = 144
ROWS = 256
COLS = 1024
RHS_COL = 896
F32 = jnp.float32
BF16 = jnp.bfloat16
MESH = pl.DeviceIdType.MESH
CHUNK = 2048
TWO = True
NT = (((1,), (1,)), ((), ()))
NN = (((1,), (0,)), ((), ()))


def moment_row(p, q):
    return 16 * p + q if p <= 4 else 80 + 8 * (p - 5) + q


def expansion():
    table = np.zeros((ROWS, COLS), np.float32)
    for k, (a, b) in enumerate(PAIRS):
        for l, (c, d) in enumerate(PAIRS):
            for p in (a + c, abs(a - c)):
                for q in (b + d, abs(b - d)):
                    table[moment_row(p, q), k * NMON + l] += 0.25
        for c in range(2):
            table[MOMENTS + c * 56 + a * 8 + b, RHS_COL + c * NMON + k] = 1.0
    return table.astype(ml_dtypes.bfloat16)


def coefficient_spread():
    table = np.zeros((112, 2 * NMON), np.float32)
    for k, (a, b) in enumerate(PAIRS):
        for c in range(2):
            table[c * 56 + a * 8 + b, c * NMON + k] = 1.0
    return table.astype(ml_dtypes.bfloat16)


def split3(x):
    high = x.astype(BF16)
    rest = x - high.astype(F32)
    middle = rest.astype(BF16)
    return high, middle, (rest - middle.astype(F32)).astype(BF16)


def dot(a, b, dims):
    return lax.dot_general(a, b, dims, preferred_element_type=F32)


def three(total, rows):
    return total[:rows] + total[rows : 2 * rows] + total[2 * rows : 3 * rows]


def widen(scale, visits, packed, expand_ref, blocks_ref, rhs_ref):
    turned = packed.T
    left = jnp.concatenate(split3(turned[:visits]), axis=0)
    right = jnp.concatenate(split3(turned[visits:]), axis=0)
    result = three(
        dot(left, expand_ref[:128, :], NN) + dot(right, expand_ref[128:, :], NN), visits
    )
    blocks_ref[...] = result[:, : NMON * NMON] * scale
    ends = jnp.concatenate([result[:, RHS_COL:]] * 2, axis=0).T
    rhs_ref[...] = ends[: 2 * NMON, :visits] * math.sqrt(scale)


def expand_kernel(
    scale,
    visits,
    total_hbm,
    offset_hbm,
    expand_hbm,
    blocks_ref,
    rhs_ref,
    offset_out,
    total_ref,
    expand_ref,
    sems,
):
    copies = [
        pltpu.make_async_copy(source, target, sems.at[i])
        for i, (source, target) in enumerate(
            ((total_hbm, total_ref), (expand_hbm, expand_ref), (offset_hbm, offset_out))
        )
    ]
    for copy in copies:
        copy.start()
    for copy in copies[:2]:
        copy.wait()
    widen(scale, visits, total_ref[...], expand_ref, blocks_ref, rhs_ref)
    copies[2].wait()


def kernel(n_dev, n_patch, scale, *refs):
    sources, refs = refs[:9], refs[9:]
    if TWO:
        (total_ref, offset_ref), refs = refs[:2], refs[2:]
    else:
        (blocks_ref, rhs_ref, offset_ref), refs = refs[:3], refs[3:]
    held, refs = refs[:9], refs[9:]
    plane_ref, weight_ref, visit_ref, holder_ref, star_ref, coef_ref, loc_ref, spread_ref, expand_ref = held
    tu_ref, tv_ref, loc_tile, part_ref, part_in, table_ref, moment_ref, moment_in, sum_ref, load_sem = refs[:10]
    send_a, recv_a, send_b, recv_b, send_c, recv_c, send_d, recv_d = refs[10:]
    loads = [
        pltpu.make_async_copy(source, target, load_sem.at[i])
        for i, (source, target) in enumerate(zip(sources, held))
        if i < 8 or not TWO
    ]
    for load in loads:
        load.start()
    me_d = lax.axis_index("dev")
    me_p = lax.axis_index("patch")
    barrier = pltpu.get_barrier_semaphore()
    for j in range(1, n_dev):
        pl.semaphore_signal(
            barrier, inc=1, device_id={"dev": lax.rem(me_d + j, n_dev)}, device_id_type=MESH
        )
    for j in range(1, n_patch):
        pl.semaphore_signal(
            barrier, inc=1, device_id={"patch": lax.rem(me_p + j, n_patch)}, device_id_type=MESH
        )
    for load in loads[:8]:
        load.wait()

    rows = weight_ref.shape[1]
    visits = coef_ref.shape[1]
    weight = weight_ref[...]
    coords = plane_ref[...]
    series = [jnp.ones_like(coords), coords]
    for degree in range(2, 13):
        series.append(2.0 * coords * series[-1] - series[-2])
    tv_ref[...] = jnp.zeros_like(tv_ref)
    for degree, value in enumerate(series):
        tu_ref[degree : degree + 1, :] = value[0:1]
        tv_ref[degree : degree + 1, :] = value[1:2]

    coef = jnp.concatenate(
        [dot(spread_ref[...], piece, NN) for piece in split3(coef_ref[...])], axis=0
    ).astype(BF16)
    width = min(CHUNK, rows)
    sub = lax.broadcasted_iota(jnp.int32, (8, width), 0)
    half = lax.div(sub, 4)
    kind = lax.rem(sub, 4)
    sums = jnp.zeros((8 * n_dev, 128), F32)
    kept = []
    for start in range(0, rows, width):
        at = slice(start, start + width)

        def basis(a, group, at=at):
            return tu_ref[a : a + 1, at] * tv_ref[8 * group : 8 * group + 8, at]

        visit_hot = jnp.where(
            lax.broadcasted_iota(jnp.int32, (visits, width), 0) == visit_ref[:, at], 1.0, 0.0
        ).astype(BF16)
        picked = three(dot(coef, visit_hot, NN), 112)
        predicted = []
        for c in range(2):
            total = picked[c * 56 : c * 56 + 8] * basis(0, 0)
            for a in range(1, 7):
                total = total + picked[c * 56 + 8 * a : c * 56 + 8 * a + 8] * basis(a, 0)
            predicted.append(jnp.sum(total, axis=0, keepdims=True))
        star = star_ref[:, at]
        weight = weight_ref[:, at]
        place = holder_ref[:, at] * 2 + lax.div(star, 128)
        low_hot = jnp.where(
            lax.broadcasted_iota(jnp.int32, (128, width), 0) == lax.rem(star, 128), 1.0, 0.0
        ).astype(BF16)
        values = jnp.where(
            kind == 0,
            weight,
            jnp.where(
                kind == 1,
                weight * predicted[0],
                jnp.where(kind == 2, weight * predicted[1], 0.0),
            ),
        )
        here = place - half
        masked = []
        for piece in split3(values):
            piece = piece.astype(F32)
            masked += [jnp.where(here == 2 * d, piece, 0.0) for d in range(n_dev)]
        sums = sums + three(
            dot(jnp.concatenate(masked, axis=0).astype(BF16), low_hot, NT), 8 * n_dev
        )
        kept.append((basis, visit_hot, low_hot, predicted, weight, here))
    for d in range(n_dev):
        part_ref[d] = sums[8 * d : 8 * d + 8]
    loc_tile[...] = jnp.zeros_like(loc_tile)
    for h in range(2):
        for c in range(2):
            loc_tile[4 * h + 1 + c : 4 * h + 2 + c, :] = loc_ref[
                c : c + 1, 128 * h : 128 * h + 128
            ]

    pl.semaphore_wait(barrier, n_dev + n_patch - 2)
    scatter = []
    for j in range(1, n_dev):
        peer = lax.rem(me_d + j, n_dev)
        copy = pltpu.make_async_remote_copy(
            src_ref=part_ref.at[peer],
            dst_ref=part_in.at[j - 1],
            send_sem=send_a.at[j - 1],
            recv_sem=recv_a.at[j - 1],
            device_id={"dev": peer},
            device_id_type=MESH,
        )
        copy.start()
        scatter.append(copy)
    star_total = part_ref[me_d]
    for j in range(1, n_dev):
        scatter[j - 1].wait_recv()
        star_total = star_total + part_in[j - 1]

    tile_row = lax.broadcasted_iota(jnp.int32, (8, 128), 0)
    mass = jnp.where(tile_row < 4, star_total[0:1], star_total[4:5])
    floor = jnp.maximum(mass, 1.0)
    location = loc_tile[...]
    offset = (star_total - mass * location) / floor
    table_ref[me_d] = jnp.where(
        lax.rem(tile_row, 4) == 0, 1.0 / floor, location + offset
    )
    gather = []
    for j in range(1, n_dev):
        copy = pltpu.make_async_remote_copy(
            src_ref=table_ref.at[me_d],
            dst_ref=table_ref.at[me_d],
            send_sem=send_b.at[j - 1],
            recv_sem=recv_b.at[j - 1],
            device_id={"dev": lax.rem(me_d + j, n_dev)},
            device_id_type=MESH,
        )
        copy.start()
        gather.append(copy)
    for h in range(2):
        for c in range(2):
            offset_ref[c : c + 1, 128 * h : 128 * h + 128] = offset[
                4 * h + 1 + c : 4 * h + 2 + c
            ]
    for copy in gather:
        copy.wait_recv()
    table = table_ref[...].reshape(8 * n_dev, 128)
    table = jnp.concatenate(split3(table), axis=0)
    wide = jnp.zeros((MOMENTS, visits), F32)
    side = jnp.zeros((ROWS - MOMENTS, visits), F32)
    for basis, visit_hot, low_hot, predicted, weight, here in kept:
        found = three(dot(table, low_hot, NN), 8 * n_dev)
        chosen = jnp.where(here == 0, found[0:8], 0.0)
        for d in range(1, n_dev):
            chosen = chosen + jnp.where(here == 2 * d, found[8 * d : 8 * d + 8], 0.0)
        chosen = chosen[0:4] + chosen[4:8]
        normal = weight * (1.0 - weight * chosen[0:1])
        error = [weight * (predicted[c] - chosen[1 + c : 2 + c]) for c in range(2)]
        stack = []
        for a in range(13):
            stack += [normal * basis(a, group) for group in range(2 if a <= 4 else 1)]
        pieces = split3(jnp.concatenate(stack, axis=0))[:2]
        stack = []
        for c in range(2):
            stack += [error[c] * basis(a, 0) for a in range(7)]
        pieces += split3(jnp.concatenate(stack, axis=0))
        both = dot(jnp.concatenate(pieces, axis=0), visit_hot, NT)
        wide = wide + both[:MOMENTS] + both[MOMENTS : 2 * MOMENTS]
        side = side + three(both[2 * MOMENTS :], ROWS - MOMENTS)
    moments = jnp.concatenate([wide, side], axis=0)
    packed = jnp.concatenate([moments[:128], moments[128:]], axis=1)
    share = 128 // n_patch
    for q in range(n_patch):
        moment_ref[q] = packed[q * share : (q + 1) * share]
    scatter_p = []
    for j in range(1, n_patch):
        peer = lax.rem(me_p + j, n_patch)
        copy = pltpu.make_async_remote_copy(
            src_ref=moment_ref.at[peer],
            dst_ref=moment_in.at[j - 1],
            send_sem=send_c.at[j - 1],
            recv_sem=recv_c.at[j - 1],
            device_id={"patch": peer},
            device_id_type=MESH,
        )
        copy.start()
        scatter_p.append(copy)
    total = moment_ref[me_p]
    for j in range(1, n_patch):
        scatter_p[j - 1].wait_recv()
        total = total + moment_in[j - 1]
    sum_ref[me_p] = total
    gather_p = []
    for j in range(1, n_patch):
        copy = pltpu.make_async_remote_copy(
            src_ref=sum_ref.at[me_p],
            dst_ref=sum_ref.at[me_p],
            send_sem=send_d.at[j - 1],
            recv_sem=recv_d.at[j - 1],
            device_id={"patch": lax.rem(me_p + j, n_patch)},
            device_id_type=MESH,
        )
        copy.start()
        gather_p.append(copy)
    if not TWO:
        loads[8].wait()
    for copy in gather_p:
        copy.wait_recv()
    if TWO:
        total_ref[...] = sum_ref[...].reshape(128, 128)
    else:
        widen(scale, visits, sum_ref[...].reshape(128, 128), expand_ref, blocks_ref, rhs_ref)
    for copy in scatter + gather + scatter_p + gather_p:
        copy.wait_send()


def per_device(n_dev, n_patch, plane, weight, visit, holder, star, coef, loc):
    rows = weight.shape[0]
    visits = coef.shape[0]
    scale = visits / (rows * n_patch)
    share = 128 // n_patch
    vmem = pl.BlockSpec(memory_space=pltpu.VMEM)
    dma = pltpu.SemaphoreType.DMA
    args = (
        plane,
        weight.reshape(1, rows),
        visit.reshape(1, rows),
        holder.reshape(1, rows),
        star.reshape(1, rows),
        coef.T,
        loc,
        jnp.asarray(coefficient_spread()),
        jnp.asarray(expansion()),
    )
    final = (
        jax.ShapeDtypeStruct((visits, NMON * NMON), F32),
        jax.ShapeDtypeStruct((2 * NMON, visits), F32),
        jax.ShapeDtypeStruct(loc.shape, F32),
    )
    first = (jax.ShapeDtypeStruct((128, 128), F32), final[2]) if TWO else final
    outs = pl.pallas_call(
        functools.partial(kernel, n_dev, n_patch, scale),
        out_shape=first,
        in_specs=[pl.BlockSpec(memory_space=pltpu.HBM)] * 9,
        out_specs=(vmem,) * len(first),
        scratch_shapes=[pltpu.VMEM(x.shape, x.dtype) for x in args]
        + [
            pltpu.VMEM((16, rows), F32),
            pltpu.VMEM((16, rows), F32),
            pltpu.VMEM((8, 128), F32),
            pltpu.VMEM((n_dev, 8, 128), F32),
            pltpu.VMEM((n_dev - 1, 8, 128), F32),
            pltpu.VMEM((n_dev, 8, 128), F32),
            pltpu.VMEM((n_patch, share, 128), F32),
            pltpu.VMEM((n_patch - 1, share, 128), F32),
            pltpu.VMEM((n_patch, share, 128), F32),
            dma((9,)),
        ]
        + [dma((n_dev - 1,))] * 4
        + [dma((n_patch - 1,))] * 4,
        compiler_params=pltpu.CompilerParams(
            collective_id=0, has_side_effects=True, vmem_limit_bytes=62 * 1024 * 1024
        ),
    )(*args)
    if TWO:
        outs = pl.pallas_call(
            functools.partial(expand_kernel, scale, visits),
            out_shape=final,
            in_specs=[pl.BlockSpec(memory_space=pltpu.HBM)] * 3,
            out_specs=(vmem, vmem, pl.BlockSpec(memory_space=pltpu.HBM)),
            scratch_shapes=[
                pltpu.VMEM((128, 128), F32),
                pltpu.VMEM((ROWS, COLS), BF16),
                dma((3,)),
            ],
            compiler_params=pltpu.CompilerParams(vmem_limit_bytes=62 * 1024 * 1024),
        )(outs[0], outs[1], args[8])
    return outs[0], outs[1].T, outs[2]


def solution(mesh):
    placed = (
        P(None, ("patch", "dev")),
        P(("patch", "dev")),
        P(("patch", "dev")),
        P(("patch", "dev"), None),
        P(("patch", "dev")),
        P("dev", None),
        P(None, ("patch", "dev")),
    )
    return jax.shard_map(
        functools.partial(per_device, mesh.shape["dev"], mesh.shape["patch"]),
        mesh=mesh,
        in_specs=placed,
        out_specs=(P("dev", None), P("dev", None), P(None, ("patch", "dev"))),
        check_vma=False,
    )
```

time: 28 us -> 24.8 us (0.89)
  local copies, waits for them, and re-layouts: 5.26 us -> 0 us
  Pallas kernels: 21.7 us -> 23.9 us
    unnamed x19 -> x0, local copies, waits for them, and re-layouts: 4.57 us -> none
    pallas_call x0 -> x1, Pallas kernels: none -> 2.28 us  [per_device(): pl.pallas_call(functools.partial(expand_kernel, scale, visits), out_shape...]
    pallas_call x1 -> x0, local copies, waits for them, and re-layouts: 0.69 us -> none  [per_device(): pl.pallas_call(functools.partial(kernel, n_dev, n_patch, scale), out_shap...]
where the time goes in v1:
time: 24.8 us; the launch traced here: 24.5 us
  Pallas kernels  23.9 us (96%)
  between operations  0.64 us (3%)
    pallas_call x1, Pallas kernels, per_device(): pl.pallas_call(functools.partial(kernel, n_dev, n_patch, scale), out_shap...  21.6 us
    pallas_call x1, Pallas kernels, per_device(): pl.pallas_call(functools.partial(expand_kernel, scale, visits), out_shape...  2.28 us

profile of v1, /device:TPU:0, one launch (start us, length us, event | category | flops | bytes accessed | tf_op | source)
XLA Modules:
  0.0 24.5 jit_solution(298446198199023873)
XLA Ops:
  0.6 21.6 %shard_map.112 = (f32[128,128]{1,0:T(8,128)}, f32[2,256]{1,0:T(2,128)}) custom-call(f32[2,2048]{1,0:T(2,128)} %refs_0_.1, f32[1,2048]{1,0:T(1,128)} %bitcast.7, s32[1,2048]{1,0:T(1,128)} %bitcast.8, s32[1,2048]{1,0:T(1,128)} %bitcast.9, s32[1,2048]{1,0:T(1,128)} %bitcast.10, f32[56,64]{1,0:T(8,128)} %bitcast.6, f32[2,256]{1,0:T(2,128)} %refs_6_.1, ...), custom_call_target="tpu_custom_call" | custom-call | tf_op jit(solution)/shard_map/pallas_call | solution.py:348
  22.3 2.3 %shard_map.113 = (f32[64,784]{1,0:T(8,128)}, f32[56,64]{1,0:T(8,128)}, f32[2,256]{1,0:T(2,128)}) custom-call(f32[128,128]{1,0:T(8,128)} %get-tuple-element.8.total_hbm, f32[2,256]{1,0:T(2,128)} %get-tuple-element.9.offset_hbm, bf16[256,1024]{1,0:T(8,128)(2,1)} %constant.5.clone.refs_8_.expand_hbm), custom_call_target="tpu_custom_call" | custom-call | tf_op jit(solution)/shard_map/pallas_call | solution.py:373

commit v2 on v1

--- a/solution.py
+++ b/solution.py
@@ -21,7 +21,6 @@
 BF16 = jnp.bfloat16
 MESH = pl.DeviceIdType.MESH
 CHUNK = 2048
-TWO = True
 NT = (((1,), (1,)), ((), ()))
 NN = (((1,), (0,)), ((), ()))
 
@@ -30,15 +29,35 @@
     return 16 * p + q if p <= 4 else 80 + 8 * (p - 5) + q
 
 
+HALF = 80
+
+
+def packing():
+    runs, end = [], 0
+    for p in range(13):
+        runs.append((end, moment_row(p, 0), 13 - p))
+        end += 13 - p
+    for c in range(2):
+        for a in range(DEG + 1):
+            runs.append((end, MOMENTS + c * 56 + a * 8, DEG + 1 - a))
+            end += DEG + 1 - a
+    return runs, end
+
+
 def expansion():
+    place = np.zeros((ROWS,), np.int32)
+    for to, source, count in packing()[0]:
+        for i in range(count):
+            row = to + i
+            place[source + i] = row if row < HALF else 128 + row - HALF
     table = np.zeros((ROWS, COLS), np.float32)
     for k, (a, b) in enumerate(PAIRS):
         for l, (c, d) in enumerate(PAIRS):
             for p in (a + c, abs(a - c)):
                 for q in (b + d, abs(b - d)):
-                    table[moment_row(p, q), k * NMON + l] += 0.25
-        for c in range(2):
-            table[MOMENTS + c * 56 + a * 8 + b, RHS_COL + c * NMON + k] = 1.0
+                    table[place[moment_row(p, q)], k * NMON + l] += 0.25
+        for c in range(2):
+            table[place[MOMENTS + c * 56 + a * 8 + b], RHS_COL + c * NMON + k] = 1.0
     return table.astype(ml_dtypes.bfloat16)
 
 
@@ -66,7 +85,7 @@
 
 
 def widen(scale, visits, packed, expand_ref, blocks_ref, rhs_ref):
-    turned = packed.T
+    turned = jnp.concatenate([packed, jnp.zeros((128 - HALF, 128), F32)], axis=0).T
     left = jnp.concatenate(split3(turned[:visits]), axis=0)
     right = jnp.concatenate(split3(turned[visits:]), axis=0)
     result = three(
@@ -104,20 +123,16 @@
     copies[2].wait()
 
 
-def kernel(n_dev, n_patch, scale, *refs):
-    sources, refs = refs[:9], refs[9:]
-    if TWO:
-        (total_ref, offset_ref), refs = refs[:2], refs[2:]
-    else:
-        (blocks_ref, rhs_ref, offset_ref), refs = refs[:3], refs[3:]
-    held, refs = refs[:9], refs[9:]
-    plane_ref, weight_ref, visit_ref, holder_ref, star_ref, coef_ref, loc_ref, spread_ref, expand_ref = held
-    tu_ref, tv_ref, loc_tile, part_ref, part_in, table_ref, moment_ref, moment_in, sum_ref, load_sem = refs[:10]
-    send_a, recv_a, send_b, recv_b, send_c, recv_c, send_d, recv_d = refs[10:]
+def kernel(n_dev, n_patch, *refs):
+    sources, refs = refs[:8], refs[8:]
+    (total_ref, offset_ref), refs = refs[:2], refs[2:]
+    held, refs = refs[:8], refs[8:]
+    plane_ref, weight_ref, visit_ref, holder_ref, star_ref, coef_ref, loc_ref, spread_ref = held
+    tu_ref, tv_ref, loc_tile, part_ref, shift_ref, line_ref, moment_ref, load_sem = refs[:8]
+    send_a, recv_a, send_c, recv_c = refs[8:]
     loads = [
         pltpu.make_async_copy(source, target, load_sem.at[i])
         for i, (source, target) in enumerate(zip(sources, held))
-        if i < 8 or not TWO
     ]
     for load in loads:
         load.start()
@@ -132,7 +147,7 @@
         pl.semaphore_signal(
             barrier, inc=1, device_id={"patch": lax.rem(me_p + j, n_patch)}, device_id_type=MESH
         )
-    for load in loads[:8]:
+    for load in loads:
         load.wait()
 
     rows = weight_ref.shape[1]
@@ -197,7 +212,7 @@
         )
         kept.append((basis, visit_hot, low_hot, predicted, weight, here))
     for d in range(n_dev):
-        part_ref[d] = sums[8 * d : 8 * d + 8]
+        part_ref[me_d, d] = sums[8 * d : 8 * d + 8]
     loc_tile[...] = jnp.zeros_like(loc_tile)
     for h in range(2):
         for c in range(2):
@@ -206,52 +221,42 @@
             ]
 
     pl.semaphore_wait(barrier, n_dev + n_patch - 2)
-    scatter = []
-    for j in range(1, n_dev):
-        peer = lax.rem(me_d + j, n_dev)
-        copy = pltpu.make_async_remote_copy(
-            src_ref=part_ref.at[peer],
-            dst_ref=part_in.at[j - 1],
-            send_sem=send_a.at[j - 1],
-            recv_sem=recv_a.at[j - 1],
-            device_id={"dev": peer},
-            device_id_type=MESH,
-        )
-        copy.start()
-        scatter.append(copy)
-    star_total = part_ref[me_d]
-    for j in range(1, n_dev):
-        scatter[j - 1].wait_recv()
-        star_total = star_total + part_in[j - 1]
-
-    tile_row = lax.broadcasted_iota(jnp.int32, (8, 128), 0)
-    mass = jnp.where(tile_row < 4, star_total[0:1], star_total[4:5])
-    floor = jnp.maximum(mass, 1.0)
-    location = loc_tile[...]
-    offset = (star_total - mass * location) / floor
-    table_ref[me_d] = jnp.where(
-        lax.rem(tile_row, 4) == 0, 1.0 / floor, location + offset
-    )
+    part_ref[me_d, n_dev] = loc_tile[...]
     gather = []
     for j in range(1, n_dev):
         copy = pltpu.make_async_remote_copy(
-            src_ref=table_ref.at[me_d],
-            dst_ref=table_ref.at[me_d],
-            send_sem=send_b.at[j - 1],
-            recv_sem=recv_b.at[j - 1],
+            src_ref=part_ref.at[me_d],
+            dst_ref=part_ref.at[me_d],
+            send_sem=send_a.at[j - 1],
+            recv_sem=recv_a.at[j - 1],
             device_id={"dev": lax.rem(me_d + j, n_dev)},
             device_id_type=MESH,
         )
         copy.start()
         gather.append(copy)
+    for copy in gather:
+        copy.wait_recv()
+    tile_row = lax.broadcasted_iota(jnp.int32, (8, 128), 0)
+    tiles = []
+    for d in range(n_dev):
+        star_total = part_ref[0, d]
+        for g in range(1, n_dev):
+            star_total = star_total + part_ref[g, d]
+        mass = jnp.where(tile_row < 4, star_total[0:1], star_total[4:5])
+        floor = jnp.maximum(mass, 1.0)
+        location = part_ref[d, n_dev]
+        offset = (star_total - mass * location) / floor
+        shift_ref[d] = offset
+        tiles.append(
+            jnp.where(lax.rem(tile_row, 4) == 0, 1.0 / floor, location + offset)
+        )
+    table = jnp.concatenate(tiles, axis=0)
+    offset = shift_ref[me_d]
     for h in range(2):
         for c in range(2):
             offset_ref[c : c + 1, 128 * h : 128 * h + 128] = offset[
                 4 * h + 1 + c : 4 * h + 2 + c
             ]
-    for copy in gather:
-        copy.wait_recv()
-    table = table_ref[...].reshape(8 * n_dev, 128)
     table = jnp.concatenate(split3(table), axis=0)
     wide = jnp.zeros((MOMENTS, visits), F32)
     side = jnp.zeros((ROWS - MOMENTS, visits), F32)
@@ -275,49 +280,29 @@
         wide = wide + both[:MOMENTS] + both[MOMENTS : 2 * MOMENTS]
         side = side + three(both[2 * MOMENTS :], ROWS - MOMENTS)
     moments = jnp.concatenate([wide, side], axis=0)
-    packed = jnp.concatenate([moments[:128], moments[128:]], axis=1)
-    share = 128 // n_patch
-    for q in range(n_patch):
-        moment_ref[q] = packed[q * share : (q + 1) * share]
-    scatter_p = []
+    line_ref[2 * HALF - 16 :, :] = jnp.zeros((16, visits), F32)
+    for to, source, count in packing()[0]:
+        line_ref[to : to + count, :] = moments[source : source + count]
+    moment_ref[me_p] = jnp.concatenate([line_ref[:HALF, :], line_ref[HALF:, :]], axis=1)
+    spread = []
     for j in range(1, n_patch):
-        peer = lax.rem(me_p + j, n_patch)
         copy = pltpu.make_async_remote_copy(
-            src_ref=moment_ref.at[peer],
-            dst_ref=moment_in.at[j - 1],
+            src_ref=moment_ref.at[me_p],
+            dst_ref=moment_ref.at[me_p],
             send_sem=send_c.at[j - 1],
             recv_sem=recv_c.at[j - 1],
-            device_id={"patch": peer},
-            device_id_type=MESH,
-        )
-        copy.start()
-        scatter_p.append(copy)
-    total = moment_ref[me_p]
-    for j in range(1, n_patch):
-        scatter_p[j - 1].wait_recv()
-        total = total + moment_in[j - 1]
-    sum_ref[me_p] = total
-    gather_p = []
-    for j in range(1, n_patch):
-        copy = pltpu.make_async_remote_copy(
-            src_ref=sum_ref.at[me_p],
-            dst_ref=sum_ref.at[me_p],
-            send_sem=send_d.at[j - 1],
-            recv_sem=recv_d.at[j - 1],
             device_id={"patch": lax.rem(me_p + j, n_patch)},
             device_id_type=MESH,
         )
         copy.start()
-        gather_p.append(copy)
-    if not TWO:
-        loads[8].wait()
-    for copy in gather_p:
+        spread.append(copy)
+    for copy in spread:
         copy.wait_recv()
-    if TWO:
-        total_ref[...] = sum_ref[...].reshape(128, 128)
-    else:
-        widen(scale, visits, sum_ref[...].reshape(128, 128), expand_ref, blocks_ref, rhs_ref)
-    for copy in scatter + gather + scatter_p + gather_p:
+    total = moment_ref[0]
+    for p in range(1, n_patch):
+        total = total + moment_ref[p]
+    total_ref[...] = total
+    for copy in gather + spread:
         copy.wait_send()
 
 
@@ -325,7 +310,6 @@
     rows = weight.shape[0]
     visits = coef.shape[0]
     scale = visits / (rows * n_patch)
-    share = 128 // n_patch
     vmem = pl.BlockSpec(memory_space=pltpu.VMEM)
     dma = pltpu.SemaphoreType.DMA
     args = (
@@ -344,44 +328,41 @@
         jax.ShapeDtypeStruct((2 * NMON, visits), F32),
         jax.ShapeDtypeStruct(loc.shape, F32),
     )
-    first = (jax.ShapeDtypeStruct((128, 128), F32), final[2]) if TWO else final
+    first = (jax.ShapeDtypeStruct((HALF, 128), F32), final[2])
     outs = pl.pallas_call(
-        functools.partial(kernel, n_dev, n_patch, scale),
+        functools.partial(kernel, n_dev, n_patch),
         out_shape=first,
-        in_specs=[pl.BlockSpec(memory_space=pltpu.HBM)] * 9,
+        in_specs=[pl.BlockSpec(memory_space=pltpu.HBM)] * 8,
         out_specs=(vmem,) * len(first),
-        scratch_shapes=[pltpu.VMEM(x.shape, x.dtype) for x in args]
+        scratch_shapes=[pltpu.VMEM(x.shape, x.dtype) for x in args[:8]]
         + [
             pltpu.VMEM((16, rows), F32),
             pltpu.VMEM((16, rows), F32),
             pltpu.VMEM((8, 128), F32),
+            pltpu.VMEM((n_dev, n_dev + 1, 8, 128), F32),
             pltpu.VMEM((n_dev, 8, 128), F32),
-            pltpu.VMEM((n_dev - 1, 8, 128), F32),
-            pltpu.VMEM((n_dev, 8, 128), F32),
-            pltpu.VMEM((n_patch, share, 128), F32),
-            pltpu.VMEM((n_patch - 1, share, 128), F32),
-            pltpu.VMEM((n_patch, share, 128), F32),
-            dma((9,)),
+            pltpu.VMEM((2 * HALF, visits), F32),
+            pltpu.VMEM((n_patch, HALF, 128), F32),
+            dma((8,)),
         ]
-        + [dma((n_dev - 1,))] * 4
-        + [dma((n_patch - 1,))] * 4,
+        + [dma((n_dev - 1,))] * 2
+        + [dma((n_patch - 1,))] * 2,
         compiler_params=pltpu.CompilerParams(
             collective_id=0, has_side_effects=True, vmem_limit_bytes=62 * 1024 * 1024
         ),
-    )(*args)
-    if TWO:
-        outs = pl.pallas_call(
-            functools.partial(expand_kernel, scale, visits),
-            out_shape=final,
-            in_specs=[pl.BlockSpec(memory_space=pltpu.HBM)] * 3,
-            out_specs=(vmem, vmem, pl.BlockSpec(memory_space=pltpu.HBM)),
-            scratch_shapes=[
-                pltpu.VMEM((128, 128), F32),
-                pltpu.VMEM((ROWS, COLS), BF16),
-                dma((3,)),
-            ],
-            compiler_params=pltpu.CompilerParams(vmem_limit_bytes=62 * 1024 * 1024),
-        )(outs[0], outs[1], args[8])
+    )(*args[:8])
+    outs = pl.pallas_call(
+        functools.partial(expand_kernel, scale, visits),
+        out_shape=final,
+        in_specs=[pl.BlockSpec(memory_space=pltpu.HBM)] * 3,
+        out_specs=(vmem, vmem, pl.BlockSpec(memory_space=pltpu.HBM)),
+        scratch_shapes=[
+            pltpu.VMEM((HALF, 128), F32),
+            pltpu.VMEM((ROWS, COLS), BF16),
+            dma((3,)),
+        ],
+        compiler_params=pltpu.CompilerParams(vmem_limit_bytes=62 * 1024 * 1024),
+    )(outs[0], outs[1], args[8])
     return outs[0], outs[1].T, outs[2]
 
 

time: 24.8 us -> 20.4 us (0.82)
  Pallas kernels: 23.9 us -> 19.5 us
    pallas_call x1, Pallas kernels: 21.6 us -> 17.2 us  [per_device(): pl.pallas_call(functools.partial(kernel, n_dev, n_patch), out_shape=first...]
where the time goes in v2:
time: 20.4 us; the launch traced here: 20.1 us
  Pallas kernels  19.5 us (96%)
  between operations  0.64 us (3%)
    pallas_call x1, Pallas kernels, per_device(): pl.pallas_call(functools.partial(kernel, n_dev, n_patch), out_shape=first...  17.2 us
    pallas_call x1, Pallas kernels, per_device(): pl.pallas_call(functools.partial(expand_kernel, scale, visits), out_shape...  2.27 us

profile of v2, /device:TPU:0, one launch (start us, length us, event | category | flops | bytes accessed | tf_op | source)
XLA Modules:
  0.0 20.1 jit_solution(7398128115168574897)
XLA Ops:
  0.6 17.2 %shard_map.112 = (f32[80,128]{1,0:T(8,128)}, f32[2,256]{1,0:T(2,128)}) custom-call(f32[2,2048]{1,0:T(2,128)} %refs_0_.1, f32[1,2048]{1,0:T(1,128)} %bitcast.7, s32[1,2048]{1,0:T(1,128)} %bitcast.8, s32[1,2048]{1,0:T(1,128)} %bitcast.9, s32[1,2048]{1,0:T(1,128)} %bitcast.10, f32[56,64]{1,0:T(8,128)} %bitcast.6, f32[2,256]{1,0:T(2,128)} %refs_6_.1, ...), custom_call_target="tpu_custom_call" | custom-call | tf_op jit(solution)/shard_map/pallas_call | solution.py:332
  17.9 2.3 %shard_map.113 = (f32[64,784]{1,0:T(8,128)}, f32[56,64]{1,0:T(8,128)}, f32[2,256]{1,0:T(2,128)}) custom-call(f32[80,128]{1,0:T(8,128)} %get-tuple-element.8.total_hbm, f32[2,256]{1,0:T(2,128)} %get-tuple-element.9.offset_hbm, bf16[256,1024]{1,0:T(8,128)(2,1)} %constant.5.clone.expand_hbm), custom_call_target="tpu_custom_call" | custom-call | tf_op jit(solution)/shard_map/pallas_call | solution.py:354

commit v3 on v2

--- a/solution.py
+++ b/solution.py
@@ -86,11 +86,8 @@
 
 def widen(scale, visits, packed, expand_ref, blocks_ref, rhs_ref):
     turned = jnp.concatenate([packed, jnp.zeros((128 - HALF, 128), F32)], axis=0).T
-    left = jnp.concatenate(split3(turned[:visits]), axis=0)
-    right = jnp.concatenate(split3(turned[visits:]), axis=0)
-    result = three(
-        dot(left, expand_ref[:128, :], NN) + dot(right, expand_ref[128:, :], NN), visits
-    )
+    joined = jnp.concatenate([turned[:visits], turned[visits:]], axis=1)
+    result = three(dot(jnp.concatenate(split3(joined), axis=0), expand_ref[...], NN), visits)
     blocks_ref[...] = result[:, : NMON * NMON] * scale
     ends = jnp.concatenate([result[:, RHS_COL:]] * 2, axis=0).T
     rhs_ref[...] = ends[: 2 * NMON, :visits] * math.sqrt(scale)
@@ -128,8 +125,8 @@
     (total_ref, offset_ref), refs = refs[:2], refs[2:]
     held, refs = refs[:8], refs[8:]
     plane_ref, weight_ref, visit_ref, holder_ref, star_ref, coef_ref, loc_ref, spread_ref = held
-    tu_ref, tv_ref, loc_tile, part_ref, shift_ref, line_ref, moment_ref, load_sem = refs[:8]
-    send_a, recv_a, send_c, recv_c = refs[8:]
+    tu_ref, tv_ref, part_ref, shift_ref, line_ref, moment_ref, load_sem = refs[:7]
+    send_a, recv_a, send_c, recv_c = refs[7:]
     loads = [
         pltpu.make_async_copy(source, target, load_sem.at[i])
         for i, (source, target) in enumerate(zip(sources, held))
@@ -213,15 +210,11 @@
         kept.append((basis, visit_hot, low_hot, predicted, weight, here))
     for d in range(n_dev):
         part_ref[me_d, d] = sums[8 * d : 8 * d + 8]
-    loc_tile[...] = jnp.zeros_like(loc_tile)
     for h in range(2):
         for c in range(2):
-            loc_tile[4 * h + 1 + c : 4 * h + 2 + c, :] = loc_ref[
-                c : c + 1, 128 * h : 128 * h + 128
-            ]
+            part_ref[me_d, 2 * h + c, 3:4, :] = loc_ref[c : c + 1, 128 * h : 128 * h + 128]
 
     pl.semaphore_wait(barrier, n_dev + n_patch - 2)
-    part_ref[me_d, n_dev] = loc_tile[...]
     gather = []
     for j in range(1, n_dev):
         copy = pltpu.make_async_remote_copy(
@@ -238,13 +231,15 @@
         copy.wait_recv()
     tile_row = lax.broadcasted_iota(jnp.int32, (8, 128), 0)
     tiles = []
+    none = jnp.zeros((1, 128), F32)
     for d in range(n_dev):
         star_total = part_ref[0, d]
         for g in range(1, n_dev):
             star_total = star_total + part_ref[g, d]
         mass = jnp.where(tile_row < 4, star_total[0:1], star_total[4:5])
         floor = jnp.maximum(mass, 1.0)
-        location = part_ref[d, n_dev]
+        near = [part_ref[d, r, 3:4, :] for r in range(4)]
+        location = jnp.concatenate([none, *near[:2], none, none, *near[2:], none], axis=0)
         offset = (star_total - mass * location) / floor
         shift_ref[d] = offset
         tiles.append(
@@ -338,8 +333,7 @@
         + [
             pltpu.VMEM((16, rows), F32),
             pltpu.VMEM((16, rows), F32),
-            pltpu.VMEM((8, 128), F32),
-            pltpu.VMEM((n_dev, n_dev + 1, 8, 128), F32),
+            pltpu.VMEM((n_dev, n_dev, 8, 128), F32),
             pltpu.VMEM((n_dev, 8, 128), F32),
             pltpu.VMEM((2 * HALF, visits), F32),
             pltpu.VMEM((n_patch, HALF, 128), F32),

time: 20.4 us -> 20 us (0.980)
  Pallas kernels: 19.5 us -> 19.1 us
    pallas_call x1, Pallas kernels: 17.2 us -> 17 us  [per_device(): pl.pallas_call(functools.partial(kernel, n_dev, n_patch), out_shape=first...]
where the time goes in v3:
time: 20 us; the launch traced here: 19.8 us
  Pallas kernels  19.1 us (96%)
  between operations  0.64 us (3%)
    pallas_call x1, Pallas kernels, per_device(): pl.pallas_call(functools.partial(kernel, n_dev, n_patch), out_shape=first...  17 us
    pallas_call x1, Pallas kernels, per_device(): pl.pallas_call(functools.partial(expand_kernel, scale, visits), out_shape...  2.18 us

profile of v3, /device:TPU:0, one launch (start us, length us, event | category | flops | bytes accessed | tf_op | source)
XLA Modules:
  0.0 19.8 jit_solution(16523304691101268272)
XLA Ops:
  0.6 17.0 %shard_map.112 = (f32[80,128]{1,0:T(8,128)}, f32[2,256]{1,0:T(2,128)}) custom-call(f32[2,2048]{1,0:T(2,128)} %refs_0_.1, f32[1,2048]{1,0:T(1,128)} %bitcast.7, s32[1,2048]{1,0:T(1,128)} %bitcast.8, s32[1,2048]{1,0:T(1,128)} %bitcast.9, s32[1,2048]{1,0:T(1,128)} %bitcast.10, f32[56,64]{1,0:T(8,128)} %bitcast.6, f32[2,256]{1,0:T(2,128)} %refs_6_.1, ...), custom_call_target="tpu_custom_call" | custom-call | tf_op jit(solution)/shard_map/pallas_call | solution.py:327
  17.6 2.2 %shard_map.113 = (f32[64,784]{1,0:T(8,128)}, f32[56,64]{1,0:T(8,128)}, f32[2,256]{1,0:T(2,128)}) custom-call(f32[80,128]{1,0:T(8,128)} %get-tuple-element.8.total_hbm, f32[2,256]{1,0:T(2,128)} %get-tuple-element.9.offset_hbm, bf16[256,1024]{1,0:T(8,128)(2,1)} %constant.5.clone.expand_hbm), custom_call_target="tpu_custom_call" | custom-call | tf_op jit(solution)/shard_map/pallas_call | solution.py:348
